TPU v7x, 32 devices: a whole 2x2x4 slice. The times are simulated.
32 devices in a mesh: parts: 2 (over x), wide: 16 (over z, y, core).
Axes of the slice: x: 2, y: 2, z: 4, core: 2. Of those that a mesh axis runs over, the one named last changes fastest.
Arguments:
- embeddings: bfloat16 [16384, 768], P(('parts', 'wide')), parts along dimension 0, may hold values from -48 to 48
- cluster_of: int32 [16384], P(('parts', 'wide')), parts along dimension 0, may hold values from 0 to 7, as said below
- sharpness: float32 [16], P('parts'), parts along dimension 0, may hold values from 2 to 16
Outputs:
- density: float32 [16384], P(('parts', 'wide')), parts along dimension 0
There are 2 independent parts, one for each index of `parts`. A program takes and returns all parts, laid end to end along the dimension named above; each array names one. Nothing has to cross between parts.
Inputs may be any that keep to these rules, and one draw needn't show every extreme that they name: `cluster_of`: in the rows of one device no cluster occurs more than 128 times; one and the same cluster occurs exactly 128 times in the rows of every device, and every cluster occurs in the rows of every device.
All inputs are finite; a program needn't handle non-finite values.
Results may differ from a plain program's by a relative error of at most 0.0003.
Values may be sent and summed in bfloat16 or wider, within the bound.
A program may use at most 64 MiB of HBM per device.

v0:
```python
import jax
import jax.numpy as jnp
from jax import lax
from jax.sharding import PartitionSpec as P

EPSILON = 1e-06


def swapped(block, axis, bit):
    count = lax.axis_size(axis)
    route = []
    for low in range(count):
        high = low | 1 << bit
        if high != low and high < count:
            route += [(low, high), (high, low)]
    return lax.ppermute(block, axis, route)


def unit_rows(embeddings):
    values = embeddings.astype(jnp.float32)
    scaled = values * lax.rsqrt(jnp.sum(values * values, axis=1, keepdims=True) + EPSILON)
    return scaled.astype(jnp.bfloat16)


def kernel_sums(left, left_live, right, right_live, sharp_value, block_size, skip_self):
    width = left.shape[1]
    left_count = left.shape[0] // block_size
    right_count = right.shape[0] // block_size
    left_blocks = left.reshape(left_count, block_size, width)
    left_masks = left_live.reshape(left_count, block_size)
    right_blocks = right.reshape(right_count, block_size, width)
    right_masks = right_live.reshape(right_count, block_size)
    offsets = jnp.arange(block_size, dtype=jnp.int32)

    def outer_step(column_total, left_item):
        left_index, left_block, left_mask = left_item

        def inner_step(row_total, right_item):
            right_index, right_block, right_mask = right_item
            similarity = jnp.einsum(
                "ie,je->ij", left_block, right_block, preferred_element_type=jnp.float32
            )
            kernel = (
                jnp.exp(sharp_value * (similarity - 1.0)) * left_mask[:, None] * right_mask[None, :]
            )
            if skip_self:
                diagonal = (left_index * block_size + offsets)[:, None] == (
                    right_index * block_size + offsets
                )[None, :]
                kernel = jnp.where(diagonal, 0.0, kernel)
            return (row_total + jnp.sum(kernel, axis=1), jnp.sum(kernel, axis=0))

        row_total, column_part = lax.scan(
            inner_step,
            jnp.zeros((block_size,), jnp.float32),
            (jnp.arange(right_count, dtype=jnp.int32), right_blocks, right_masks),
        )
        return (column_total + column_part, row_total)

    column_total, row_totals = lax.scan(
        outer_step,
        jnp.zeros((right_count, block_size), jnp.float32),
        (jnp.arange(left_count, dtype=jnp.int32), left_blocks, left_masks),
    )
    return (row_totals.reshape(left.shape[0]), column_total.reshape(right.shape[0]))


def per_device(embeddings, cluster_of, sharpness):
    devices = lax.axis_size("wide")
    device_index = lax.axis_index("wide")
    local_rows = embeddings.shape[0]
    width = embeddings.shape[1]
    clusters = sharpness.shape[0]
    capacity = local_rows // clusters
    slots = devices * capacity
    block_size = min(512, slots // 2)
    unit_vectors = unit_rows(embeddings)
    onehot_int = (cluster_of[:, None] == jnp.arange(clusters, dtype=jnp.int32)[None, :]).astype(
        jnp.int32
    )
    within = jnp.sum((jnp.cumsum(onehot_int, axis=0) - onehot_int) * onehot_int, axis=1)
    target = 2 * cluster_of + within % 2
    position = target * capacity + within // 2
    send_rows = jnp.zeros((slots, width), jnp.bfloat16).at[position].set(unit_vectors)
    per_cluster = jnp.sum(onehot_int, axis=0)
    per_target = jnp.stack([(per_cluster + 1) // 2, per_cluster // 2], axis=1).reshape(devices)
    slot_column = jnp.arange(capacity, dtype=jnp.int32)
    own_rows, own_counts = (
        lax.all_to_all(send_rows, "wide", split_axis=0, concat_axis=0, tiled=True),
        lax.all_to_all(
            per_target.astype(jnp.bfloat16), "wide", split_axis=0, concat_axis=0, tiled=True
        ),
    )
    own_live = (
        (slot_column[None, :] < own_counts.astype(jnp.int32)[:, None])
        .astype(jnp.float32)
        .reshape(slots)
    )
    partner_rows, partner_flags = swapped((own_rows, own_live.astype(jnp.bfloat16)), "wide", 0)
    partner_live = partner_flags.astype(jnp.float32)
    sharp_value = lax.dynamic_slice_in_dim(sharpness, device_index // 2, 1, 0)[0]
    members = jnp.sum(own_live) + jnp.sum(partner_live)
    divisor = jnp.maximum(members - 1.0, 1.0)
    self_rows, unused_columns = kernel_sums(
        own_rows, own_live, own_rows, own_live, sharp_value, block_size, True
    )
    cross_rows, other_columns = kernel_sums(
        own_rows, own_live, partner_rows, partner_live, sharp_value, block_size, False
    )
    kernel_total = self_rows + cross_rows
    density_here = jnp.log((kernel_total + (1.0 - own_live)) / divisor)
    returned = lax.all_to_all(density_here, "wide", split_axis=0, concat_axis=0, tiled=True)
    return jnp.take(returned, position, axis=0)


def solution(mesh):
    in_specs = (P(("parts", "wide"), None), P(("parts", "wide")), P("parts"))
    out_specs = P(("parts", "wide"))
    return jax.shard_map(
        per_device, mesh=mesh, in_specs=in_specs, out_specs=out_specs, check_vma=False
    )
```

profile of v0, /device:TPU:0, one launch (start us, length us, event | category | flops | bytes accessed | tf_op | source)
XLA Modules:
  0.0 104.7 jit_solution(8934550447980633119)
XLA Ops:
  0.0 0.7 fusion.28
  0.7 1.1 %reduce-window.6 = s32[8,4,128]{2,0,1:T(8,128)S(1)} reduce-window(s32[8,4,128]{2,0,1:T(8,128)S(1)} %fusion.28, s32[]{:T(128)} %constant.202.clone.1), window={size=1x1x128 pad=0_0x0_0x127_0}, to_apply=%region_0.0 | reduce-window | flops 520192 | bytes 32772 | tf_op jit(solution)/shard_map/reduce-window
  2.1 0.9 convert_reduce_fusion
  3.8 7.4 %all-to-all-start.1 = ((bf16[16,1,1]{2,1,0:T(2,128)(2,1)}), bf16[16,1,1]{2,1,0:T(2,128)(2,1)S(1)}, u32[]{:S(2)}, u32[]{:S(2)}) async-start(bf16[16,1,1]{2,1,0:T(2,128)(2,1)} %convert_element_type.84), calls=%async_computation.1 | async-start | bytes 16384 | tf_op jit(solution)/shard_map/all_to_all | solution.py:90
  11.2 0.7 compare_select_fusion
  11.8 1.4 %fusion.20 = f32[512]{0:T(512)S(1)} fusion(bf16[512,768]{1,0:T(8,128)(2,1)} %param.11), kind=kLoop, calls=%fused_computation.35 | loop fusion | flops 1179136 | bytes 788480 | tf_op jit(solution)/shard_map/reduce_sum | solution.py:21
  13.2 4.5 %scatter_custom_fusion = bf16[1024,768]{1,0:T(8,128)(2,1)} fusion(s32[512]{0:T(512)S(1)} %compare_select_fusion, bf16[512,768]{1,0:T(8,128)(2,1)} %param.11, f32[512]{0:T(512)S(1)} %add_rsqrt_fusion, bf16[]{:T(256)} %constant.209.clone.1), kind=kCustom, calls=%fused_computation.37 | custom fusion | flops 1179648 | bytes 2361346 | tf_op jit(solution)/shard_map/scatter | solution.py:84
  17.7 6.2 %all-to-all-start = ((bf16[16,64,768]{2,1,0:T(8,128)(2,1)}), bf16[16,64,768]{2,1,0:T(8,128)(2,1)}, u32[]{:S(2)}, u32[]{:S(2)}) async-start(bf16[16,64,768]{2,1,0:T(8,128)(2,1)} %bitcast.6), calls=%async_computation | async-start | bytes 3145728 | tf_op jit(solution)/shard_map/all_to_all | solution.py:89
  25.7 0.8 convert_reduce_fusion.1
  28.4 27.5 %all-to-all-done = bf16[16,64,768]{2,1,0:T(8,128)(2,1)} async-done(((bf16[16,64,768]{2,1,0:T(8,128)(2,1)}), bf16[16,64,768]{2,1,0:T(8,128)(2,1)}, u32[]{:S(2)}, u32[]{:S(2)}) %all-to-all-start) | async-done | bytes 1572896 | tf_op jit(solution)/shard_map/all_to_all | solution.py:89
  55.9 0.8 collective-permute-start
  56.7 20.1 %while.76 = (s32[]{:T(128)}, f32[2,512]{1,0:T(2,128)S(1)}, bf16[2,512,768]{2,1,0:T(8,128)(2,1)}, f32[2,512]{1,0:T(2,128)S(1)}, s32[2]{0:T(128)S(1)}, /*index=5*/...) while((s32[]{:T(128)}, f32[2,512]{1,0:T(2,128)S(1)}, ...), condition=%wide.region_10.11_spmd.clone.clone, body=%wide.region_6.10_spmd.clone.clone.sunk | while | flops 404489728 | bytes 3184060 | solution.py:60
  56.7 1.2 %dynamic-slice_bitcast_fusion.5 = bf16[512,768]{1,0:T(8,128)(2,1)S(1)} fusion(bf16[2,512,768]{2,1,0:T(8,128)(2,1)} %get-tuple-element.978, s32[]{:T(128)} %get-tuple-element.964), kind=kLoop, calls=%fused_computation.31.clone.1 | loop fusion | bytes 1572868 | tf_op jit(solution)/shard_map/while/body/jit(dynamic_index_in_dim)/squeeze | solution.py:60
  59.2 7.5 %while.78 = (s32[]{:T(128)}, f32[512]{0:T(512)S(1)}, s32[]{:T(128)}, s32[512]{0:T(512)S(1)}, s32[2]{0:T(128)S(1)}, /*index=5*/f32[]{:T(128)}, bf16[2,512,768]{2,...) while((s32[]{:T(128)}, f32[512]{0:T(512)S(1)}, ...), condition=%wide.region_9.9_spmd.clone.clone, body=%wide.region_7.8_spmd.clone.clone.sunk | while | flops 404489728 | bytes 1600683 | solution.py:53
  60.5 2.5 %fusion.46 = f32[512]{0:T(512)S(1)} fusion(bf16[512,768]{1,0:T(8,128)(2,1)S(1)} %get-tuple-element.919, bf16[2,512,768]{2,1,0:T(8,128)(2,1)} %get-tuple-element.918, s32[]{:T(128)} %get-tuple-element.899, f32[512]{0:T(512)S(1)} %bitcast.85, f32[512]{0:T(512)S(1)} %get-tuple-element.920, f32[]{:T(128)} %get-tuple-element.917, ...), kind=kOutput, calls=%fused_computation.23.clone.1 | convolution fusion | flops 404487680 | bytes 1584128 | tf_op jit(solution)/shard_map/while/body/eval_jaxpr/while/body/eval_jaxpr/ie,je->ij/dot_general | solution.py:40
  64.2 2.5 %fusion.46 = f32[512]{0:T(512)S(1)} fusion(bf16[512,768]{1,0:T(8,128)(2,1)S(1)} %get-tuple-element.919, bf16[2,512,768]{2,1,0:T(8,128)(2,1)} %get-tuple-element.918, s32[]{:T(128)} %get-tuple-element.899, f32[512]{0:T(512)S(1)} %bitcast.85, f32[512]{0:T(512)S(1)} %get-tuple-element.920, f32[]{:T(128)} %get-tuple-element.917, ...), kind=kOutput, calls=%fused_computation.23.clone.1 | convolution fusion | flops 404487680 | bytes 1584128 | tf_op jit(solution)/shard_map/while/body/eval_jaxpr/while/body/eval_jaxpr/ie,je->ij/dot_general | solution.py:40
  66.8 1.2 %dynamic-slice_bitcast_fusion.5 = bf16[512,768]{1,0:T(8,128)(2,1)S(1)} fusion(bf16[2,512,768]{2,1,0:T(8,128)(2,1)} %get-tuple-element.978, s32[]{:T(128)} %get-tuple-element.964), kind=kLoop, calls=%fused_computation.31.clone.1 | loop fusion | bytes 1572868 | tf_op jit(solution)/shard_map/while/body/jit(dynamic_index_in_dim)/squeeze | solution.py:60
  69.3 7.5 %while.78 = (s32[]{:T(128)}, f32[512]{0:T(512)S(1)}, s32[]{:T(128)}, s32[512]{0:T(512)S(1)}, s32[2]{0:T(128)S(1)}, /*index=5*/f32[]{:T(128)}, bf16[2,512,768]{2,...) while((s32[]{:T(128)}, f32[512]{0:T(512)S(1)}, ...), condition=%wide.region_9.9_spmd.clone.clone, body=%wide.region_7.8_spmd.clone.clone.sunk | while | flops 404489728 | bytes 1600683 | solution.py:53
  70.6 2.5 %fusion.46 = f32[512]{0:T(512)S(1)} fusion(bf16[512,768]{1,0:T(8,128)(2,1)S(1)} %get-tuple-element.919, bf16[2,512,768]{2,1,0:T(8,128)(2,1)} %get-tuple-element.918, s32[]{:T(128)} %get-tuple-element.899, f32[512]{0:T(512)S(1)} %bitcast.85, f32[512]{0:T(512)S(1)} %get-tuple-element.920, f32[]{:T(128)} %get-tuple-element.917, ...), kind=kOutput, calls=%fused_computation.23.clone.1 | convolution fusion | flops 404487680 | bytes 1584128 | tf_op jit(solution)/shard_map/while/body/eval_jaxpr/while/body/eval_jaxpr/ie,je->ij/dot_general | solution.py:40
  74.3 2.5 %fusion.46 = f32[512]{0:T(512)S(1)} fusion(bf16[512,768]{1,0:T(8,128)(2,1)S(1)} %get-tuple-element.919, bf16[2,512,768]{2,1,0:T(8,128)(2,1)} %get-tuple-element.918, s32[]{:T(128)} %get-tuple-element.899, f32[512]{0:T(512)S(1)} %bitcast.85, f32[512]{0:T(512)S(1)} %get-tuple-element.920, f32[]{:T(128)} %get-tuple-element.917, ...), kind=kOutput, calls=%fused_computation.23.clone.1 | convolution fusion | flops 404487680 | bytes 1584128 | tf_op jit(solution)/shard_map/while/body/eval_jaxpr/while/body/eval_jaxpr/ie,je->ij/dot_general | solution.py:40
  76.9 7.8 %while.74 = (s32[]{:T(128)}, f32[2,512]{1,0:T(2,128)S(1)}, bf16[2,512,768]{2,1,0:T(8,128)(2,1)}, f32[2,512]{1,0:T(2,128)S(1)}, f32[]{:T(128)}, /*index=5*/bf16[2...) while((s32[]{:T(128)}, f32[2,512]{1,0:T(2,128)S(1)}, ...), condition=%wide.region_15.16_spmd, body=%wide.region_11.15_spmd.sunk | while | flops 403964416 | bytes 3170620 | solution.py:60
  76.9 1.2 %dynamic-slice_bitcast_fusion.4 = bf16[512,768]{1,0:T(8,128)(2,1)S(1)} fusion(bf16[2,512,768]{2,1,0:T(8,128)(2,1)} %get-tuple-element.1012, s32[]{:T(128)} %get-tuple-element.999), kind=kLoop, calls=%fused_computation.14.clone.1 | loop fusion | bytes 1572868 | tf_op jit(solution)/shard_map/while/body/jit(dynamic_index_in_dim)/squeeze | solution.py:60
  78.1 2.6 %while.77 = (s32[]{:T(128)}, f32[512]{0:T(512)S(1)}, f32[]{:T(128)}, bf16[2,512,768]{2,1,0:T(8,128)(2,1)S(1)}, bf16[512,768]{1,0:T(8,128)(2,1)S(1)}, /*index=5*/...) while((s32[]{:T(128)}, f32[512]{0:T(512)S(1)}, f32[]{:T(128)}, ...), condition=%wide.region_14.14_spmd.clone, body=%wide.region_12.13_spmd.clone.sunk | while | flops 403964416 | bytes 1589363 | solution.py:53
  78.1 1.3 %fusion.49 = f32[512]{0:T(512)S(1)} fusion(bf16[512,768]{1,0:T(8,128)(2,1)S(1)} %get-tuple-element.947, bf16[2,512,768]{2,1,0:T(8,128)(2,1)S(1)} %get-tuple-element.946, s32[]{:T(128)} %get-tuple-element.934, f32[512]{0:T(512)S(1)} %bitcast.86, f32[512]{0:T(512)S(1)} %get-tuple-element.948, f32[]{:T(128)} %get-tuple-element.945), kind=kOutput, calls=%fused_computation.8.clone.1 | convolution fusion | flops 403963392 | bytes 1579016 | tf_op jit(solution)/shard_map/while/body/eval_jaxpr/while/body/eval_jaxpr/ie,je->ij/dot_general | solution.py:40
  79.5 1.3 %fusion.49 = f32[512]{0:T(512)S(1)} fusion(bf16[512,768]{1,0:T(8,128)(2,1)S(1)} %get-tuple-element.947, bf16[2,512,768]{2,1,0:T(8,128)(2,1)S(1)} %get-tuple-element.946, s32[]{:T(128)} %get-tuple-element.934, f32[512]{0:T(512)S(1)} %bitcast.86, f32[512]{0:T(512)S(1)} %get-tuple-element.948, f32[]{:T(128)} %get-tuple-element.945), kind=kOutput, calls=%fused_computation.8.clone.1 | convolution fusion | flops 403963392 | bytes 1579016 | tf_op jit(solution)/shard_map/while/body/eval_jaxpr/while/body/eval_jaxpr/ie,je->ij/dot_general | solution.py:40
  80.8 1.2 %dynamic-slice_bitcast_fusion.4 = bf16[512,768]{1,0:T(8,128)(2,1)S(1)} fusion(bf16[2,512,768]{2,1,0:T(8,128)(2,1)} %get-tuple-element.1012, s32[]{:T(128)} %get-tuple-element.999), kind=kLoop, calls=%fused_computation.14.clone.1 | loop fusion | bytes 1572868 | tf_op jit(solution)/shard_map/while/body/jit(dynamic_index_in_dim)/squeeze | solution.py:60
  82.0 2.6 %while.77 = (s32[]{:T(128)}, f32[512]{0:T(512)S(1)}, f32[]{:T(128)}, bf16[2,512,768]{2,1,0:T(8,128)(2,1)S(1)}, bf16[512,768]{1,0:T(8,128)(2,1)S(1)}, /*index=5*/...) while((s32[]{:T(128)}, f32[512]{0:T(512)S(1)}, f32[]{:T(128)}, ...), condition=%wide.region_14.14_spmd.clone, body=%wide.region_12.13_spmd.clone.sunk | while | flops 403964416 | bytes 1589363 | solution.py:53
  82.1 1.3 %fusion.49 = f32[512]{0:T(512)S(1)} fusion(bf16[512,768]{1,0:T(8,128)(2,1)S(1)} %get-tuple-element.947, bf16[2,512,768]{2,1,0:T(8,128)(2,1)S(1)} %get-tuple-element.946, s32[]{:T(128)} %get-tuple-element.934, f32[512]{0:T(512)S(1)} %bitcast.86, f32[512]{0:T(512)S(1)} %get-tuple-element.948, f32[]{:T(128)} %get-tuple-element.945), kind=kOutput, calls=%fused_computation.8.clone.1 | convolution fusion | flops 403963392 | bytes 1579016 | tf_op jit(solution)/shard_map/while/body/eval_jaxpr/while/body/eval_jaxpr/ie,je->ij/dot_general | solution.py:40
  83.4 1.3 %fusion.49 = f32[512]{0:T(512)S(1)} fusion(bf16[512,768]{1,0:T(8,128)(2,1)S(1)} %get-tuple-element.947, bf16[2,512,768]{2,1,0:T(8,128)(2,1)S(1)} %get-tuple-element.946, s32[]{:T(128)} %get-tuple-element.934, f32[512]{0:T(512)S(1)} %bitcast.86, f32[512]{0:T(512)S(1)} %get-tuple-element.948, f32[]{:T(128)} %get-tuple-element.945), kind=kOutput, calls=%fused_computation.8.clone.1 | convolution fusion | flops 403963392 | bytes 1579016 | tf_op jit(solution)/shard_map/while/body/eval_jaxpr/while/body/eval_jaxpr/ie,je->ij/dot_general | solution.py:40
  85.5 8.6 %all-to-all-start.2 = ((f32[16,64,1]{1,2,0:T(1,128)}), f32[16,64,1]{1,2,0:T(1,128)S(1)}, u32[]{:S(2)}, u32[]{:S(2)}) async-start(f32[16,64,1]{1,2,0:T(1,128)} %bitcast.12), calls=%async_computation.2 | async-start | bytes 16384 | tf_op jit(solution)/shard_map/all_to_all | solution.py:112
  94.1 6.4 %all-to-all-done.2 = f32[16,64,1]{1,2,0:T(1,128)S(1)} async-done(((f32[16,64,1]{1,2,0:T(1,128)}), f32[16,64,1]{1,2,0:T(1,128)S(1)}, u32[]{:S(2)}, u32[]{:S(2)}) %all-to-all-start.2) | async-done | bytes 4128 | tf_op jit(solution)/shard_map/all_to_all | solution.py:112
  101.8 2.3 %gather_fusion = f32[512]{0:T(512)S(1)} fusion(f32[1024]{0:T(1024)S(1)} %all_to_all.23, s32[1024]{0:T(1024)S(1)} %pad_clamp_fusion), kind=kCustom, calls=%fused_computation | custom fusion | bytes 6144 | tf_op jit(solution)/shard_map/jit(_take)/gather | solution.py:113
  (79 shorter events, 10.2 us)
Async XLA Ops:
  3.8 14.0 %all-to-all-start.1 = ((bf16[16,1,1]{2,1,0:T(2,128)(2,1)}), bf16[16,1,1]{2,1,0:T(2,128)(2,1)S(1)}, u32[]{:S(2)}, u32[]{:S(2)}) async-start(bf16[16,1,1]{2,1,0:T(2,128)(2,1)} %convert_element_type.84), calls=%async_computation.1 | async-start | bytes 16384 | tf_op jit(solution)/shard_map/all_to_all | solution.py:90
  17.7 6.3 %copy-start = (f32[8]{0:T(128)S(1)}, f32[8]{0:T(128)}, u32[]{:S(2)}) copy-start(f32[8]{0:T(128)} %param.13) | copy-start | bytes 100
  17.7 38.2 %all-to-all-start = ((bf16[16,64,768]{2,1,0:T(8,128)(2,1)}), bf16[16,64,768]{2,1,0:T(8,128)(2,1)}, u32[]{:S(2)}, u32[]{:S(2)}) async-start(bf16[16,64,768]{2,1,0:T(8,128)(2,1)} %bitcast.6), calls=%async_computation | async-start | bytes 3145728 | tf_op jit(solution)/shard_map/all_to_all | solution.py:89
  25.3 1.2 %collective-permute-start.1 = (bf16[1024]{0:T(1024)(128)(2,1)S(1)}, bf16[1024]{0:T(1024)(128)(2,1)S(1)}, u32[]{:S(2)}, u32[]{:S(2)}) collective-permute-start(bf16[1024]{0:T(1024)(128)(2,1)S(1)} %convert_element_type.79), channel_id=1, source_target_pairs={{0,1},{1,0},{2,3},{3,2},{4,5},{5,4},{6,7},{7,6},{8,9},{9,8},{10,11... | collective-permute-start | bytes 6152 | tf_op jit(solution)/shard_map/ppermute | solution.py:16
  55.9 20.9 %collective-permute-start = (bf16[1024,768]{1,0:T(8,128)(2,1)}, bf16[1024,768]{1,0:T(8,128)(2,1)S(1)}, u32[]{:S(2)}, u32[]{:S(2)}) collective-permute-start(bf16[1024,768]{1,0:T(8,128)(2,1)} %bitcast.10), channel_id=1, source_target_pairs={{0,1},{1,0},{2,3},{3,2},{4,5},{5,4},{6,7},{7,6},{8,9},{9,8},{10,11... | collective-permute-start | bytes 4718600 | tf_op jit(solution)/shard_map/ppermute | solution.py:16
  85.5 15.1 %all-to-all-start.2 = ((f32[16,64,1]{1,2,0:T(1,128)}), f32[16,64,1]{1,2,0:T(1,128)S(1)}, u32[]{:S(2)}, u32[]{:S(2)}) async-start(f32[16,64,1]{1,2,0:T(1,128)} %bitcast.12), calls=%async_computation.2 | async-start | bytes 16384 | tf_op jit(solution)/shard_map/all_to_all | solution.py:112
where the time goes:
time: 106 us; the launch traced here: 105 us
  waiting for transfers between devices  34 us (32%)
  starting transfers between devices  23.3 us (22%)
  matrix products  14.9 us (14%)
  local copies, waits for them, and re-layouts  13.6 us (13%)
  other arithmetic  13.2 us (12%)
  loops' own time  4.19 us (4%)
  between operations  1.41 us (1%)
    all_to_all x1, waiting for transfers between devices, per_device(): lax.all_to_all(send_rows, 'wide', split_axis=0, concat_axis=0, tiled=True)  27.5 us
    dot_general x8, matrix products, inner_step(): jnp.einsum('ie,je->ij', left_block, right_block, preferred_element_type=j...  14.9 us
    all_to_all x1, starting transfers between devices, per_device(): lax.all_to_all(density_here, 'wide', split_axis=0, concat_axis=0, tiled=T...  8.63 us
    all_to_all x1, starting transfers between devices, per_device(): lax.all_to_all(per_target.astype(jnp.bfloat16), 'wide', split_axis=0, con...  7.39 us
    all_to_all x1, waiting for transfers between devices, per_device(): lax.all_to_all(density_here, 'wide', split_axis=0, concat_axis=0, tiled=T...  6.39 us
    all_to_all x1, starting transfers between devices, per_device(): lax.all_to_all(send_rows, 'wide', split_axis=0, concat_axis=0, tiled=True)  6.18 us
    squeeze x4, local copies, waits for them, and re-layouts, kernel_sums(): lax.scan(outer_step, jnp.zeros((right_count, block_size), jnp.float32), (...  4.75 us
    scatter x1, other arithmetic, per_device(): jnp.zeros((slots, width), jnp.bfloat16).at[position].set(unit_vectors)  4.49 us
  transfers between devices with their start and end apart: 5, of which 3 were waited for; matrix products, arithmetic and copies ran while one was open for 24% of the time, Pallas kernels for 0%

commit v1 on v0

v1 whole, which is shorter than its diff:
```python
import functools

import jax
import jax.numpy as jnp
from jax import lax
from jax.experimental import pallas as pl
from jax.experimental.pallas import tpu as pltpu
from jax.sharding import PartitionSpec as P

EPSILON = 1e-06
LOG2E = 1.4426950408889634
DEAD = -1e30
LANES = 128
GROUP_ROWS = 256
MESH = pl.DeviceIdType.MESH


def flipped(value, mask, bits):
    out = 0
    for k in range(bits):
        left = (value // (1 << k)) % 2
        right = (mask // (1 << k)) % 2
        out = out + (left + right - 2 * left * right) * (1 << k)
    return out


def body(
    devices, clusters, cap,
    emb_ref, cluster_ref, sharp_ref, out_ref,
    unit, send, own, other, count_out, count_in, own_bias, other_bias, total, back_out, back_in,
    row_send, row_recv, count_send, count_recv, pass_send, pass_recv, back_send, back_recv,
):
    bits = devices.bit_length() - 1
    me = lax.axis_index("wide")
    rows, width = emb_ref.shape
    fan = GROUP_ROWS // cap
    groups = devices // fan
    group_bits = groups.bit_length() - 1
    my_group = me // fan
    half = me % 2
    partner = me + 1 - 2 * half
    my_cluster = me // 2

    def peer(mask):
        return flipped(me, mask, bits)

    def group_of(mask):
        return flipped(my_group, mask, group_bits)

    barrier = pltpu.get_barrier_semaphore()
    for mask in range(1, devices):
        pl.semaphore_signal(barrier, inc=1, device_id={"wide": peer(mask)}, device_id_type=MESH)

    cluster = cluster_ref[...]
    onehot = lax.broadcasted_iota(jnp.int32, (clusters, rows), 0) == cluster
    ones = jnp.where(onehot, 1.0, 0.0)
    before = (
        lax.broadcasted_iota(jnp.int32, (rows, rows), 0)
        < lax.broadcasted_iota(jnp.int32, (rows, rows), 1)
    )
    prefix = jnp.dot(
        ones.astype(jnp.bfloat16),
        jnp.where(before, 1.0, 0.0).astype(jnp.bfloat16),
        preferred_element_type=jnp.float32,
    )
    within = jnp.sum(prefix * ones, axis=0, keepdims=True).astype(jnp.int32)
    target = 2 * cluster + (within & 1)
    place = within >> 1
    position = target * cap + place
    counts = jnp.broadcast_to(jnp.sum(ones, axis=1, keepdims=True), (clusters, LANES))
    for c in range(clusters):
        count_out[c] = jnp.broadcast_to(counts[c : c + 1], (8, LANES))

    values = emb_ref[...].astype(jnp.float32)
    scale = lax.rsqrt(jnp.sum(values * values, axis=1, keepdims=True) + EPSILON)
    unit[...] = (values * scale).astype(jnp.bfloat16)

    pl.semaphore_wait(barrier, devices - 1)

    def count_copy(mask):
        to = peer(mask)
        return pltpu.make_async_remote_copy(
            src_ref=count_out.at[to // 2], dst_ref=count_in.at[me],
            send_sem=count_send.at[mask], recv_sem=count_recv.at[mask],
            device_id={"wide": to}, device_id_type=MESH,
        )

    def row_copy(mask):
        to = peer(mask)
        return pltpu.make_async_remote_copy(
            src_ref=send.at[to], dst_ref=own.at[me],
            send_sem=row_send.at[mask], recv_sem=row_recv.at[mask],
            device_id={"wide": to}, device_id_type=MESH,
        )

    def pass_copy(mask, landing):
        origin = peer(mask)
        return pltpu.make_async_remote_copy(
            src_ref=own.at[origin], dst_ref=other.at[origin],
            send_sem=pass_send.at[mask], recv_sem=pass_recv.at[landing],
            device_id={"wide": partner}, device_id_type=MESH,
        )

    def back_copy(mask):
        to = peer(mask)
        return pltpu.make_async_remote_copy(
            src_ref=back_out.at[(to * cap) // LANES], dst_ref=back_in.at[me],
            send_sem=back_send.at[mask], recv_sem=back_recv.at[mask],
            device_id={"wide": to}, device_id_type=MESH,
        )

    for step in reversed(range(groups)):
        goal = group_of(step)
        slot = lax.broadcasted_iota(jnp.int32, (GROUP_ROWS, rows), 0) + goal * GROUP_ROWS
        pick = jnp.where(slot == position, 1.0, 0.0).astype(jnp.bfloat16)
        packed = jnp.dot(pick, unit[...], preferred_element_type=jnp.float32)
        send[pl.ds(goal * fan, fan)] = packed.astype(jnp.bfloat16).reshape(fan, cap, width)
        for g in range(fan):
            mask = step * fan + g
            if mask:
                row_copy(mask).start()
            else:
                own[me] = send[me]
        if step == groups - 1:
            for mask in range(1, devices):
                count_copy(mask).start()
    count_in[me] = count_out[my_cluster]

    sharp = sharp_ref[my_cluster] * LOG2E
    total[...] = jnp.zeros_like(total)
    inner = lax.broadcasted_iota(jnp.int32, (cap, LANES), 0).astype(jnp.float32)
    skip = (
        lax.broadcasted_iota(jnp.int32, (GROUP_ROWS, GROUP_ROWS), 0)
        == lax.broadcasted_iota(jnp.int32, (GROUP_ROWS, GROUP_ROWS), 1)
    )
    half_f = half.astype(jnp.float32)

    def add_block(rows_ref, bias_ref, j, i, diagonal=False):
        left = rows_ref[pl.ds(j * fan, fan)].reshape(GROUP_ROWS, width)
        right = own[pl.ds(i * fan, fan)].reshape(GROUP_ROWS, width)
        similarity = lax.dot_general(
            left, right, (((1,), (1,)), ((), ())), preferred_element_type=jnp.float32
        )
        bias = bias_ref[pl.ds(j * fan, fan)].reshape(GROUP_ROWS, LANES)
        bias = jnp.concatenate([bias] * (GROUP_ROWS // LANES), axis=1)
        kernel = jnp.exp2(similarity * sharp + bias)
        if diagonal:
            kernel = jnp.where(skip, 0.0, kernel)
        total[i] += jnp.sum(kernel.reshape(GROUP_ROWS // 8, 8, GROUP_ROWS), axis=0)

    for step in range(groups):
        for g in range(fan):
            mask = step * fan + g
            if mask:
                row_copy(mask).wait_recv()
            pass_copy(mask, mask ^ 1).start()
        for g in range(fan):
            mask = step * fan + g
            origin = peer(mask)
            if mask:
                count_copy(mask).wait_recv()
            count = count_in[origin][0:1]
            own_live = jnp.floor((count + 1.0 - half_f) * 0.5)
            own_bias[origin] = jnp.where(inner < own_live, -sharp, DEAD)
            other_bias[origin] = jnp.where(inner < count - own_live, -sharp, DEAD)
        here = group_of(step)
        add_block(own, own_bias, here, here, diagonal=True)
        for g in range(fan):
            pass_copy(step * fan + g, step * fan + g).wait_recv()
        add_block(other, other_bias, here, here)
        if step:

            def earlier(index, carry):
                there = group_of(index)
                add_block(own, own_bias, here, there)
                add_block(other, other_bias, here, there)
                add_block(own, own_bias, there, here)
                add_block(other, other_bias, there, here)
                return carry

            lax.fori_loop(0, step, earlier, 0)

    members = jnp.sum(count_in[...], axis=0)[0:1]
    divisor = jnp.maximum(members - 1.0, 1.0)
    pieces = GROUP_ROWS // LANES
    for i in range(groups):
        sums = jnp.sum(total[i], axis=0, keepdims=True)
        for piece in range(pieces):
            density = jnp.log(sums[:, piece * LANES : (piece + 1) * LANES] / divisor)
            back_out[i * pieces + piece] = jnp.broadcast_to(density, (8, LANES))
    for mask in range(1, devices):
        back_copy(mask).start()
    back_in[me] = back_out[(me * cap) // LANES]

    lane = place + (me * cap) % LANES
    choose = jnp.where(lax.broadcasted_iota(jnp.int32, (LANES, rows), 0) == lane, 1.0, 0.0)
    mine = lax.broadcasted_iota(jnp.int32, (devices, rows), 0) == target
    for mask in range(1, devices):
        back_copy(mask).wait_recv()
    gathered = jnp.dot(
        back_in[...][:, 0, :], choose,
        preferred_element_type=jnp.float32, precision=lax.Precision.HIGHEST,
    )
    out_ref[...] = jnp.sum(jnp.where(mine, gathered, 0.0), axis=0, keepdims=True)

    for mask in range(devices):
        pass_copy(mask, mask ^ 1).wait_send()
        if mask:
            count_copy(mask).wait_send()
            row_copy(mask).wait_send()
            back_copy(mask).wait_send()


def per_device(embeddings, cluster_of, sharpness):
    devices = lax.axis_size("wide")
    rows, width = embeddings.shape
    clusters = sharpness.shape[0]
    cap = max(16, rows // clusters)
    slots = devices * cap
    vmem = pl.BlockSpec(memory_space=pltpu.VMEM)
    dma = pltpu.SemaphoreType.DMA((devices,))
    out = pl.pallas_call(
        functools.partial(body, devices, clusters, cap),
        out_shape=jax.ShapeDtypeStruct((1, rows), jnp.float32),
        in_specs=[vmem, vmem, pl.BlockSpec(memory_space=pltpu.SMEM)],
        out_specs=vmem,
        scratch_shapes=[
            pltpu.VMEM((rows, width), jnp.bfloat16),
            pltpu.VMEM((devices, cap, width), jnp.bfloat16),
            pltpu.VMEM((devices, cap, width), jnp.bfloat16),
            pltpu.VMEM((devices, cap, width), jnp.bfloat16),
            pltpu.VMEM((clusters, 8, LANES), jnp.float32),
            pltpu.VMEM((devices, 8, LANES), jnp.float32),
            pltpu.VMEM((devices, cap, LANES), jnp.float32),
            pltpu.VMEM((devices, cap, LANES), jnp.float32),
            pltpu.VMEM((slots // GROUP_ROWS, 8, GROUP_ROWS), jnp.float32),
            pltpu.VMEM((slots // LANES, 8, LANES), jnp.float32),
            pltpu.VMEM((devices, 8, LANES), jnp.float32),
            dma, dma, dma, dma, dma, dma, dma, dma,
        ],
        compiler_params=pltpu.CompilerParams(
            collective_id=0, has_side_effects=True, vmem_limit_bytes=40 * 1024 * 1024
        ),
    )(embeddings, cluster_of.reshape(1, rows), sharpness)
    return out.reshape(rows)


def solution(mesh):
    in_specs = (P(("parts", "wide"), None), P(("parts", "wide")), P("parts"))
    out_specs = P(("parts", "wide"))
    return jax.shard_map(
        per_device, mesh=mesh, in_specs=in_specs, out_specs=out_specs, check_vma=False
    )
```

time: 106 us -> 62.7 us (0.59); the launches traced: 105 us -> 62.5 us
  Pallas kernels: 0 us -> 59.4 us
  waiting for transfers between devices: 34 us -> 0 us
  starting transfers between devices: 23.3 us -> 0 us
  matrix products: 14.9 us -> 0 us
  other arithmetic: 13.2 us -> 0 us
  local copies, waits for them, and re-layouts: 13.6 us -> 3.05 us
  loops' own time: 4.19 us -> 0 us
  between operations: 1.41 us -> 0.01 us
    pallas_call x0 -> x1, Pallas kernels: none -> 59.4 us  [per_device(): pl.pallas_call(functools.partial(body, devices, clusters, cap), out_shape...]
    all_to_all x3 -> x0, waiting for transfers between devices: 33.9 us -> none  [the longest x1 27.5 us: per_device(): lax.all_to_all(send_rows, 'wide', split_axis=0, concat_axis=0, tiled=True)]
    all_to_all x3 -> x0, starting transfers between devices: 22.2 us -> none  [the longest x1 8.63 us: per_device(): lax.all_to_all(density_here, 'wide', split_axis=0, concat_axis=0, tiled=T...]
    dot_general x8 -> x0, matrix products: 14.9 us -> none  [inner_step(): jnp.einsum('ie,je->ij', left_block, right_block, preferred_element_type=j...]
    squeeze x4 -> x0, local copies, waits for them, and re-layouts: 4.75 us -> none  [kernel_sums(): lax.scan(outer_step, jnp.zeros((right_count, block_size), jnp.float32), (...]
    scatter x1 -> x0, other arithmetic: 4.49 us -> none  [per_device(): jnp.zeros((slots, width), jnp.bfloat16).at[position].set(unit_vectors)]
    dynamic_slice x19 -> x0, local copies, waits for them, and re-layouts: 4.34 us -> none  [the longest x18 3.79 us: kernel_sums(): lax.scan(outer_step, jnp.zeros((right_count, block_size), jnp.float32), (...]
    another operation x6 -> x0, loops' own time: 4.19 us -> none  [the longest x4 2.73 us: outer_step(): lax.scan(inner_step, jnp.zeros((block_size,), jnp.float32), (jnp.arange(r...]
  transfers between devices with their start and end apart: 5 -> 0, of which waited for: 3 -> 0; matrix products, arithmetic and copies ran while one was open for 24% -> 0% of each run, Pallas kernels for 0% -> 0%
where the time goes in v1:
time: 62.7 us; the launch traced here: 62.5 us
  Pallas kernels  59.4 us (95%)
  local copies, waits for them, and re-layouts  3.05 us (5%)
    pallas_call x1, Pallas kernels, per_device(): pl.pallas_call(functools.partial(body, devices, clusters, cap), out_shape...  59.4 us
    unnamed x7, local copies, waits for them, and re-layouts  3.05 us

profile of v1, /device:TPU:0, one launch (start us, length us, event | category | flops | bytes accessed | tf_op | source)
XLA Modules:
  0.0 62.5 jit_solution(7410833834161352489)
XLA Ops:
  0.0 0.0 copy-start.2
  0.0 0.7 %copy-done.2 = f32[8]{0:T(128)S(1)} copy-done((f32[8]{0:T(128)S(1)}, f32[8]{0:T(128)}, u32[]{:S(2)}) %copy-start.2) | copy-done | bytes 56
  0.7 0.0 copy-start
  0.7 1.1 %copy-done = bf16[512,768]{1,0:T(8,128)(2,1)S(1)} copy-done((bf16[512,768]{1,0:T(8,128)(2,1)S(1)}, bf16[512,768]{1,0:T(8,128)(2,1)}, u32[]{:S(2)}) %copy-start) | copy-done | bytes 786456
  1.8 0.0 copy-start.1
  1.8 0.7 %copy-done.1 = s32[512]{0:T(512)S(1)} copy-done((s32[512]{0:T(512)S(1)}, s32[512]{0:T(512)}, u32[]{:S(2)}) %copy-start.1) | copy-done | bytes 2072
  2.5 59.4 %shard_map.37 = f32[1,512]{1,0:T(1,128)S(1)} custom-call(bf16[512,768]{1,0:T(8,128)(2,1)S(1)} %copy-done, s32[1,512]{1,0:T(1,128)S(1)} %bitcast.3, f32[8]{0:T(128)S(1)} %copy-done.2), custom_call_target="tpu_custom_call" | custom-call | tf_op jit(solution)/shard_map/pallas_call | solution.py:222
  61.9 0.6 copy.5
Async XLA Ops:
  0.0 0.7 %copy-start.2 = (f32[8]{0:T(128)S(1)}, f32[8]{0:T(128)}, u32[]{:S(2)}) copy-start(f32[8]{0:T(128)} %sharp_ref.1) | copy-start | bytes 100
  0.7 1.1 %copy-start = (bf16[512,768]{1,0:T(8,128)(2,1)S(1)}, bf16[512,768]{1,0:T(8,128)(2,1)}, u32[]{:S(2)}) copy-start(bf16[512,768]{1,0:T(8,128)(2,1)} %emb_ref.1) | copy-start | bytes 2359300
  1.8 0.7 %copy-start.1 = (s32[512]{0:T(512)S(1)}, s32[512]{0:T(512)}, u32[]{:S(2)}) copy-start(s32[512]{0:T(512)} %param.4) | copy-start | bytes 6148

commit v2 on v1

--- a/solution.py
+++ b/solution.py
@@ -13,6 +13,8 @@
 LANES = 128
 GROUP_ROWS = 256
 MESH = pl.DeviceIdType.MESH
+RANK_CAPS = (64, 64, 64, 64, 48, 48, 32, 32)
+RANK_PLACES = (0, 4, 5, 1, 2, 6, 3, 7)
 
 
 def flipped(value, mask, bits):
@@ -25,10 +27,12 @@
 
 
 def body(
-    devices, clusters, cap,
-    emb_ref, cluster_ref, sharp_ref, out_ref,
-    unit, send, own, other, count_out, count_in, own_bias, other_bias, total, back_out, back_in,
+    devices, clusters, cap, caps, places,
+    emb_ref, cluster_ref, sharp_ref, out_ref, flag_ref,
+    unit, send, own, other, count_out, count_in, home_count, own_bias, other_bias, total,
+    back_out, back_in, flag_out, flag_in,
     row_send, row_recv, count_send, count_recv, pass_send, pass_recv, back_send, back_recv,
+    flag_send, flag_recv,
 ):
     bits = devices.bit_length() - 1
     me = lax.axis_index("wide")
@@ -39,7 +43,24 @@
     my_group = me // fan
     half = me % 2
     partner = me + 1 - 2 * half
-    my_cluster = me // 2
+    my_place = me // 2
+    twin = {"parts": 1 - lax.axis_index("parts")}
+    sizes = sorted(set(caps))
+    adaptive = places is not None
+
+    def size_at(place):
+        out = 0
+        for rank, size in enumerate(caps):
+            out = out + jnp.where(place == places[rank], size, 0)
+        return out
+
+    def with_size(place, act):
+        if not adaptive:
+            act(cap)
+            return
+        size = size_at(place)
+        for case in sizes:
+            pl.when(size == case)(functools.partial(act, case))
 
     def peer(mask):
         return flipped(me, mask, bits)
@@ -47,7 +68,17 @@
     def group_of(mask):
         return flipped(my_group, mask, group_bits)
 
+    if adaptive:
+        least = sizes[0]
+
+        @pl.when(size_at(my_place) < cap)
+        def clear():
+            for ref in (own, other):
+                ref[:, least:, :] = jnp.zeros((devices, cap - least, width), jnp.bfloat16)
+
     barrier = pltpu.get_barrier_semaphore()
+    if adaptive:
+        pl.semaphore_signal(barrier, inc=1, device_id=twin, device_id_type=MESH)
     for mask in range(1, devices):
         pl.semaphore_signal(barrier, inc=1, device_id={"wide": peer(mask)}, device_id_type=MESH)
 
@@ -64,39 +95,73 @@
         preferred_element_type=jnp.float32,
     )
     within = jnp.sum(prefix * ones, axis=0, keepdims=True).astype(jnp.int32)
-    target = 2 * cluster + (within & 1)
     place = within >> 1
-    position = target * cap + place
-    counts = jnp.broadcast_to(jnp.sum(ones, axis=1, keepdims=True), (clusters, LANES))
-    for c in range(clusters):
-        count_out[c] = jnp.broadcast_to(counts[c : c + 1], (8, LANES))
+    count_out[...] = jnp.broadcast_to(jnp.sum(ones, axis=1, keepdims=True), (clusters, LANES))
+    count_in[me] = count_out[...]
+    pl.semaphore_wait(barrier, devices if adaptive else devices - 1)
+
+    def count_copy(mask):
+        return pltpu.make_async_remote_copy(
+            src_ref=count_out, dst_ref=count_in.at[me],
+            send_sem=count_send.at[mask], recv_sem=count_recv.at[mask],
+            device_id={"wide": peer(mask)}, device_id_type=MESH,
+        )
+
+    for mask in reversed(range(1, devices)):
+        count_copy(mask).start()
 
     values = emb_ref[...].astype(jnp.float32)
     scale = lax.rsqrt(jnp.sum(values * values, axis=1, keepdims=True) + EPSILON)
     unit[...] = (values * scale).astype(jnp.bfloat16)
 
-    pl.semaphore_wait(barrier, devices - 1)
-
-    def count_copy(mask):
+    for mask in range(1, devices):
+        count_copy(mask).wait_recv()
+    cluster_id = lax.broadcasted_iota(jnp.int32, (clusters, LANES), 0)
+    flag_copy = pltpu.make_async_remote_copy(
+        src_ref=flag_out, dst_ref=flag_in, send_sem=flag_send, recv_sem=flag_recv,
+        device_id=twin, device_id_type=MESH,
+    )
+    if adaptive:
+        most = jnp.max(count_in[...], axis=0)
+        rank = jnp.zeros((clusters, LANES), jnp.int32)
+        for c in range(clusters):
+            against = most[c : c + 1]
+            ahead = (against > most) | ((against == most) & (cluster_id > c))
+            rank = rank + jnp.where(ahead, 1, 0)
+        home = jnp.zeros((clusters, LANES), jnp.int32)
+        room = jnp.zeros((clusters, LANES), jnp.float32)
+        for r in range(clusters):
+            home = home + jnp.where(rank == r, places[r], 0)
+            room = room + jnp.where(rank == r, 2.0 * caps[r], 0.0)
+        excess = jnp.max(jnp.where(most > room, 1.0, 0.0), axis=0, keepdims=True)
+        flag_out[...] = jnp.broadcast_to(excess, (8, LANES))
+        flag_copy.start()
+        wide_home = jnp.concatenate([home] * (rows // LANES), axis=1)
+        label = jnp.sum(jnp.where(onehot, wide_home, 0), axis=0, keepdims=True)
+    else:
+        home = cluster_id
+        label = cluster
+    target = 2 * label + (within & 1)
+    position = target * cap + place
+    at_home = home == my_place
+    home_count[...] = jnp.broadcast_to(
+        jnp.sum(jnp.where(at_home, count_in[...], 0.0), axis=1, keepdims=True),
+        (devices, 8, LANES),
+    )
+    sharp = LOG2E * jnp.sum(jnp.where(at_home, sharp_ref[...], 0.0), axis=0, keepdims=True)
+
+    def row_copy(mask, size):
         to = peer(mask)
         return pltpu.make_async_remote_copy(
-            src_ref=count_out.at[to // 2], dst_ref=count_in.at[me],
-            send_sem=count_send.at[mask], recv_sem=count_recv.at[mask],
-            device_id={"wide": to}, device_id_type=MESH,
-        )
-
-    def row_copy(mask):
-        to = peer(mask)
-        return pltpu.make_async_remote_copy(
-            src_ref=send.at[to], dst_ref=own.at[me],
+            src_ref=send.at[to, pl.ds(0, size)], dst_ref=own.at[me, pl.ds(0, size)],
             send_sem=row_send.at[mask], recv_sem=row_recv.at[mask],
             device_id={"wide": to}, device_id_type=MESH,
         )
 
-    def pass_copy(mask, landing):
+    def pass_copy(mask, landing, size):
         origin = peer(mask)
         return pltpu.make_async_remote_copy(
-            src_ref=own.at[origin], dst_ref=other.at[origin],
+            src_ref=own.at[origin, pl.ds(0, size)], dst_ref=other.at[origin, pl.ds(0, size)],
             send_sem=pass_send.at[mask], recv_sem=pass_recv.at[landing],
             device_id={"wide": partner}, device_id_type=MESH,
         )
@@ -118,15 +183,11 @@
         for g in range(fan):
             mask = step * fan + g
             if mask:
-                row_copy(mask).start()
+                with_size(peer(mask) // 2, lambda size: row_copy(mask, size).start())
             else:
                 own[me] = send[me]
-        if step == groups - 1:
-            for mask in range(1, devices):
-                count_copy(mask).start()
-    count_in[me] = count_out[my_cluster]
-
-    sharp = sharp_ref[my_cluster] * LOG2E
+
+    wide_sharp = jnp.concatenate([sharp] * (GROUP_ROWS // LANES), axis=1)
     total[...] = jnp.zeros_like(total)
     inner = lax.broadcasted_iota(jnp.int32, (cap, LANES), 0).astype(jnp.float32)
     skip = (
@@ -143,30 +204,36 @@
         )
         bias = bias_ref[pl.ds(j * fan, fan)].reshape(GROUP_ROWS, LANES)
         bias = jnp.concatenate([bias] * (GROUP_ROWS // LANES), axis=1)
-        kernel = jnp.exp2(similarity * sharp + bias)
+        kernel = jnp.exp2(similarity * wide_sharp + bias)
         if diagonal:
             kernel = jnp.where(skip, 0.0, kernel)
         total[i] += jnp.sum(kernel.reshape(GROUP_ROWS // 8, 8, GROUP_ROWS), axis=0)
 
     for step in range(groups):
-        for g in range(fan):
-            mask = step * fan + g
-            if mask:
-                row_copy(mask).wait_recv()
-            pass_copy(mask, mask ^ 1).start()
+
+        def land(size):
+            for g in range(fan):
+                mask = step * fan + g
+                if mask:
+                    row_copy(mask, size).wait_recv()
+                pass_copy(mask, mask ^ 1, size).start()
+
+        with_size(my_place, land)
         for g in range(fan):
             mask = step * fan + g
             origin = peer(mask)
-            if mask:
-                count_copy(mask).wait_recv()
-            count = count_in[origin][0:1]
+            count = home_count[origin][0:1]
             own_live = jnp.floor((count + 1.0 - half_f) * 0.5)
             own_bias[origin] = jnp.where(inner < own_live, -sharp, DEAD)
             other_bias[origin] = jnp.where(inner < count - own_live, -sharp, DEAD)
         here = group_of(step)
         add_block(own, own_bias, here, here, diagonal=True)
-        for g in range(fan):
-            pass_copy(step * fan + g, step * fan + g).wait_recv()
+
+        def passed(size):
+            for g in range(fan):
+                pass_copy(step * fan + g, step * fan + g, size).wait_recv()
+
+        with_size(my_place, passed)
         add_block(other, other_bias, here, here)
         if step:
 
@@ -180,7 +247,7 @@
 
             lax.fori_loop(0, step, earlier, 0)
 
-    members = jnp.sum(count_in[...], axis=0)[0:1]
+    members = jnp.sum(home_count[...], axis=0)[0:1]
     divisor = jnp.maximum(members - 1.0, 1.0)
     pieces = GROUP_ROWS // LANES
     for i in range(groups):
@@ -203,12 +270,127 @@
     )
     out_ref[...] = jnp.sum(jnp.where(mine, gathered, 0.0), axis=0, keepdims=True)
 
-    for mask in range(devices):
-        pass_copy(mask, mask ^ 1).wait_send()
-        if mask:
-            count_copy(mask).wait_send()
-            row_copy(mask).wait_send()
-            back_copy(mask).wait_send()
+    def passed_on(size):
+        for mask in range(devices):
+            pass_copy(mask, mask ^ 1, size).wait_send()
+
+    with_size(my_place, passed_on)
+    for mask in range(1, devices):
+        count_copy(mask).wait_send()
+        with_size(peer(mask) // 2, lambda size: row_copy(mask, size).wait_send())
+        back_copy(mask).wait_send()
+    if adaptive:
+        flag_copy.wait()
+        flag_ref[...] = jnp.maximum(flag_out[...], flag_in[...])
+    else:
+        flag_ref[...] = jnp.zeros((8, LANES), jnp.float32)
+
+
+def swapped(block, axis, bit):
+    count = lax.axis_size(axis)
+    route = []
+    for low in range(count):
+        high = low | 1 << bit
+        if high != low and high < count:
+            route += [(low, high), (high, low)]
+    return lax.ppermute(block, axis, route)
+
+
+def unit_rows(embeddings):
+    values = embeddings.astype(jnp.float32)
+    scaled = values * lax.rsqrt(jnp.sum(values * values, axis=1, keepdims=True) + EPSILON)
+    return scaled.astype(jnp.bfloat16)
+
+
+def kernel_sums(left, left_live, right, right_live, sharp_value, block_size, skip_self):
+    width = left.shape[1]
+    left_count = left.shape[0] // block_size
+    right_count = right.shape[0] // block_size
+    left_blocks = left.reshape(left_count, block_size, width)
+    left_masks = left_live.reshape(left_count, block_size)
+    right_blocks = right.reshape(right_count, block_size, width)
+    right_masks = right_live.reshape(right_count, block_size)
+    offsets = jnp.arange(block_size, dtype=jnp.int32)
+
+    def outer_step(column_total, left_item):
+        left_index, left_block, left_mask = left_item
+
+        def inner_step(row_total, right_item):
+            right_index, right_block, right_mask = right_item
+            similarity = jnp.einsum(
+                "ie,je->ij", left_block, right_block, preferred_element_type=jnp.float32
+            )
+            kernel = (
+                jnp.exp(sharp_value * (similarity - 1.0)) * left_mask[:, None] * right_mask[None, :]
+            )
+            if skip_self:
+                diagonal = (left_index * block_size + offsets)[:, None] == (
+                    right_index * block_size + offsets
+                )[None, :]
+                kernel = jnp.where(diagonal, 0.0, kernel)
+            return (row_total + jnp.sum(kernel, axis=1), jnp.sum(kernel, axis=0))
+
+        row_total, column_part = lax.scan(
+            inner_step,
+            jnp.zeros((block_size,), jnp.float32),
+            (jnp.arange(right_count, dtype=jnp.int32), right_blocks, right_masks),
+        )
+        return (column_total + column_part, row_total)
+
+    column_total, row_totals = lax.scan(
+        outer_step,
+        jnp.zeros((right_count, block_size), jnp.float32),
+        (jnp.arange(left_count, dtype=jnp.int32), left_blocks, left_masks),
+    )
+    return (row_totals.reshape(left.shape[0]), column_total.reshape(right.shape[0]))
+
+
+def any_counts(embeddings, cluster_of, sharpness):
+    devices = lax.axis_size("wide")
+    device_index = lax.axis_index("wide")
+    local_rows = embeddings.shape[0]
+    width = embeddings.shape[1]
+    clusters = sharpness.shape[0]
+    capacity = local_rows // clusters
+    slots = devices * capacity
+    block_size = min(512, slots // 2)
+    unit_vectors = unit_rows(embeddings)
+    onehot_int = (cluster_of[:, None] == jnp.arange(clusters, dtype=jnp.int32)[None, :]).astype(
+        jnp.int32
+    )
+    within = jnp.sum((jnp.cumsum(onehot_int, axis=0) - onehot_int) * onehot_int, axis=1)
+    target = 2 * cluster_of + within % 2
+    position = target * capacity + within // 2
+    send_rows = jnp.zeros((slots, width), jnp.bfloat16).at[position].set(unit_vectors)
+    per_cluster = jnp.sum(onehot_int, axis=0)
+    per_target = jnp.stack([(per_cluster + 1) // 2, per_cluster // 2], axis=1).reshape(devices)
+    slot_column = jnp.arange(capacity, dtype=jnp.int32)
+    own_rows, own_counts = (
+        lax.all_to_all(send_rows, "wide", split_axis=0, concat_axis=0, tiled=True),
+        lax.all_to_all(
+            per_target.astype(jnp.bfloat16), "wide", split_axis=0, concat_axis=0, tiled=True
+        ),
+    )
+    own_live = (
+        (slot_column[None, :] < own_counts.astype(jnp.int32)[:, None])
+        .astype(jnp.float32)
+        .reshape(slots)
+    )
+    partner_rows, partner_flags = swapped((own_rows, own_live.astype(jnp.bfloat16)), "wide", 0)
+    partner_live = partner_flags.astype(jnp.float32)
+    sharp_value = lax.dynamic_slice_in_dim(sharpness, device_index // 2, 1, 0)[0]
+    members = jnp.sum(own_live) + jnp.sum(partner_live)
+    divisor = jnp.maximum(members - 1.0, 1.0)
+    self_rows, unused_columns = kernel_sums(
+        own_rows, own_live, own_rows, own_live, sharp_value, block_size, True
+    )
+    cross_rows, other_columns = kernel_sums(
+        own_rows, own_live, partner_rows, partner_live, sharp_value, block_size, False
+    )
+    kernel_total = self_rows + cross_rows
+    density_here = jnp.log((kernel_total + (1.0 - own_live)) / divisor)
+    returned = lax.all_to_all(density_here, "wide", split_axis=0, concat_axis=0, tiled=True)
+    return jnp.take(returned, position, axis=0)
 
 
 def per_device(embeddings, cluster_of, sharpness):
@@ -219,30 +401,48 @@
     slots = devices * cap
     vmem = pl.BlockSpec(memory_space=pltpu.VMEM)
     dma = pltpu.SemaphoreType.DMA((devices,))
-    out = pl.pallas_call(
-        functools.partial(body, devices, clusters, cap),
-        out_shape=jax.ShapeDtypeStruct((1, rows), jnp.float32),
-        in_specs=[vmem, vmem, pl.BlockSpec(memory_space=pltpu.SMEM)],
-        out_specs=vmem,
+    adaptive = clusters == len(RANK_CAPS) and cap == max(RANK_CAPS)
+    caps = RANK_CAPS if adaptive else (cap,) * clusters
+    places = RANK_PLACES if adaptive else None
+    out, flag = pl.pallas_call(
+        functools.partial(body, devices, clusters, cap, caps, places),
+        out_shape=(
+            jax.ShapeDtypeStruct((1, rows), jnp.float32),
+            jax.ShapeDtypeStruct((8, LANES), jnp.float32),
+        ),
+        in_specs=[vmem, vmem, vmem],
+        out_specs=(vmem, vmem),
         scratch_shapes=[
             pltpu.VMEM((rows, width), jnp.bfloat16),
             pltpu.VMEM((devices, cap, width), jnp.bfloat16),
             pltpu.VMEM((devices, cap, width), jnp.bfloat16),
             pltpu.VMEM((devices, cap, width), jnp.bfloat16),
-            pltpu.VMEM((clusters, 8, LANES), jnp.float32),
+            pltpu.VMEM((clusters, LANES), jnp.float32),
+            pltpu.VMEM((devices, clusters, LANES), jnp.float32),
             pltpu.VMEM((devices, 8, LANES), jnp.float32),
             pltpu.VMEM((devices, cap, LANES), jnp.float32),
             pltpu.VMEM((devices, cap, LANES), jnp.float32),
             pltpu.VMEM((slots // GROUP_ROWS, 8, GROUP_ROWS), jnp.float32),
             pltpu.VMEM((slots // LANES, 8, LANES), jnp.float32),
             pltpu.VMEM((devices, 8, LANES), jnp.float32),
+            pltpu.VMEM((8, LANES), jnp.float32),
+            pltpu.VMEM((8, LANES), jnp.float32),
             dma, dma, dma, dma, dma, dma, dma, dma,
+            pltpu.SemaphoreType.DMA, pltpu.SemaphoreType.DMA,
         ],
         compiler_params=pltpu.CompilerParams(
             collective_id=0, has_side_effects=True, vmem_limit_bytes=40 * 1024 * 1024
         ),
-    )(embeddings, cluster_of.reshape(1, rows), sharpness)
-    return out.reshape(rows)
+    )(embeddings, cluster_of.reshape(1, rows), sharpness.reshape(clusters, 1))
+    out = out.reshape(rows)
+    if not adaptive:
+        return out
+    return lax.cond(
+        flag[0, 0] > 0.0,
+        lambda values, ids, sharp, ready: any_counts(values, ids, sharp),
+        lambda values, ids, sharp, ready: ready,
+        embeddings, cluster_of, sharpness, out,
+    )
 
 
 def solution(mesh):

time: 62.7 us -> 58 us (0.925)
  Pallas kernels: 59.4 us -> 55.1 us
  local copies, waits for them, and re-layouts: 3.05 us -> 1.82 us
  between operations: 0.01 us -> 0.67 us
    pallas_call x1, Pallas kernels: 59.4 us -> 55.1 us  [per_device(): pl.pallas_call(functools.partial(body, devices, clusters, cap, caps, plac...]
    unnamed x7 -> x1, local copies, waits for them, and re-layouts: 3.05 us -> 0.58 us
    reshape x0 -> x1, local copies, waits for them, and re-layouts: none -> 0.73 us  [per_device(): sharpness.reshape(clusters, 1)]
where the time goes in v2:
time: 58 us; the launch traced here: 57.9 us
  Pallas kernels  55.1 us (95%)
  local copies, waits for them, and re-layouts  1.82 us (3%)
  between operations  0.67 us (1%)
    pallas_call x1, Pallas kernels, per_device(): pl.pallas_call(functools.partial(body, devices, clusters, cap, caps, plac...  55.1 us

profile of v2, /device:TPU:0, one launch (start us, length us, event | category | flops | bytes accessed | tf_op | source)
XLA Modules:
  0.0 57.9 jit_solution(3154216777025632056)
XLA Ops:
  0.0 0.7 %copy.22.sharp_ref = f32[8,1]{1,0:T(8,128)S(1)} copy(f32[8,1]{0,1:T(1,128)} %bitcast.96) | data formatting | bytes 64 | tf_op jit(solution)/shard_map/reshape | solution.py:436
  0.7 55.1 %shard_map.39 = (f32[1,512]{1,0:T(1,128)S(1)}, f32[8,128]{1,0:T(8,128)S(1)}) custom-call(bf16[512,768]{1,0:T(8,128)(2,1)} %emb_ref.1, s32[1,512]{1,0:T(1,128)} %bitcast.93, f32[8,1]{1,0:T(8,128)S(1)} %copy.22.sharp_ref), custom_call_target="tpu_custom_call" | custom-call | tf_op jit(solution)/shard_map/pallas_call | solution.py:407
  55.9 0.5 slice.9
  57.1 0.2 conditional.1
  57.3 0.6 %copy.52 = f32[512]{0:T(512)} copy(f32[512]{0:T(512)S(1)} %get-tuple-element.484) | data formatting | bytes 4096

commit v3 on v2

--- a/solution.py
+++ b/solution.py
@@ -174,7 +174,7 @@
             device_id={"wide": to}, device_id_type=MESH,
         )
 
-    for step in reversed(range(groups)):
+    for step in ((2, 3, 1, 0) if groups == 4 else reversed(range(groups))):
         goal = group_of(step)
         slot = lax.broadcasted_iota(jnp.int32, (GROUP_ROWS, rows), 0) + goal * GROUP_ROWS
         pick = jnp.where(slot == position, 1.0, 0.0).astype(jnp.bfloat16)

time: 58 us -> 55 us (0.948)
  Pallas kernels: 55.1 us -> 52.2 us
    pallas_call x1, Pallas kernels: 55.1 us -> 52.2 us  [per_device(): pl.pallas_call(functools.partial(body, devices, clusters, cap, caps, plac...]
where the time goes in v3:
time: 55 us; the launch traced here: 54.9 us
  Pallas kernels  52.2 us (95%)
  local copies, waits for them, and re-layouts  1.82 us (3%)
  between operations  0.67 us (1%)
    pallas_call x1, Pallas kernels, per_device(): pl.pallas_call(functools.partial(body, devices, clusters, cap, caps, plac...  52.2 us

profile of v3, /device:TPU:0, one launch (start us, length us, event | category | flops | bytes accessed | tf_op | source)
XLA Modules:
  0.0 54.9 jit_solution(3997990843492572615)
XLA Ops:
  0.0 0.7 %copy.22.sharp_ref = f32[8,1]{1,0:T(8,128)S(1)} copy(f32[8,1]{0,1:T(1,128)} %bitcast.96) | data formatting | bytes 64 | tf_op jit(solution)/shard_map/reshape | solution.py:436
  0.7 52.2 %shard_map.39 = (f32[1,512]{1,0:T(1,128)S(1)}, f32[8,128]{1,0:T(8,128)S(1)}) custom-call(bf16[512,768]{1,0:T(8,128)(2,1)} %emb_ref.1, s32[1,512]{1,0:T(1,128)} %bitcast.93, f32[8,1]{1,0:T(8,128)S(1)} %copy.22.sharp_ref), custom_call_target="tpu_custom_call" | custom-call | tf_op jit(solution)/shard_map/pallas_call | solution.py:407
  52.9 0.5 slice.9
  54.1 0.2 conditional.1
  54.3 0.6 %copy.52 = f32[512]{0:T(512)} copy(f32[512]{0:T(512)S(1)} %get-tuple-element.484) | data formatting | bytes 4096
